TPU v7x, 32 devices: a whole 2x2x4 slice. The times are simulated.
32 devices in a mesh: dp: 4 (over y, x), seq: 8 (over z, core).
Axes of the slice: x: 2, y: 2, z: 4, core: 2. Of those that a mesh axis runs over, the one named last changes fastest.
Arguments:
- query_tok: bfloat16 [4, 1024, 2560], P('dp', 'seq'), may hold values from -6 to 6
- key_tok: bfloat16 [4, 1024, 2560], P('dp', 'seq'), may hold values from -6 to 6
- value_tok: bfloat16 [4, 1024, 2560], P('dp', 'seq'), may hold values from -6 to 6
- grad_out: bfloat16 [4, 1024, 5120], P('dp', 'seq'), may hold values from -6 to 6
- out_weight: bfloat16 [24, 128, 5120], P('seq', None, 'dp'), may hold values from -0.125 to 0.125
- block_mask: int32 [20, 8, 8], replicated, may hold values from 0 to 1, as said below
- head_owner: int32 [20], replicated, may hold values from 0 to 7, as said below
Outputs:
- attn_out: bfloat16 [4, 1024, 2560], P('dp', 'seq')
- query_grad: bfloat16 [4, 1024, 2560], P('dp', 'seq')
- key_grad: bfloat16 [4, 1024, 2560], P('dp', 'seq')
- value_grad: bfloat16 [4, 1024, 2560], P('dp', 'seq')
- weight_grad: float32 [24, 128, 5120], P('seq', None, 'dp')
Inputs may be any that keep to these rules, and one draw needn't show every extreme that they name: `block_mask`: every diagonal tile is 1; each head has its own share of other tiles. `head_owner`: each value is an index of seq; no index holds more than 3 heads, and some index holds exactly 3.
All inputs are finite; a program needn't handle non-finite values.
Results may differ from a plain program's by a relative error of at most 0.017.
Values may be sent and summed in bfloat16 or wider, within the bound.
A program may use at most 128 MiB of HBM per device.

v0:
```python
import functools

import jax
import jax.numpy as jnp
from jax import lax
from jax.experimental import pallas as pl
from jax.experimental.pallas import tpu as pltpu
from jax.sharding import PartitionSpec as P

F32 = jnp.float32
BF16 = jnp.bfloat16
NT = (((1,), (1,)), ((), ()))
TN = (((0,), (0,)), ((), ()))
NN = (((1,), (0,)), ((), ()))


def dot(a, b, dims):
    return lax.dot_general(a, b, dims, preferred_element_type=F32)


def slot_numbers(head_owner, most):
    count = head_owner.shape[0]
    same = head_owner[:, None] == head_owner[None, :]
    earlier = jnp.arange(count)[None, :] < jnp.arange(count)[:, None]
    rank = jnp.sum(jnp.logical_and(same, earlier), axis=1).astype(jnp.int32)
    return head_owner * most + rank


def forward_kernel(scale, bias_ref, qkv_ref, out_ref, lse_ref):
    blocks, rows, dim = qkv_ref.shape[0], qkv_ref.shape[3], qkv_ref.shape[4]
    keys = qkv_ref[:, 0, 1].reshape(blocks * rows, dim)
    values = qkv_ref[:, 0, 2].reshape(blocks * rows, dim)
    slot = pl.program_id(0)

    @pl.loop(0, blocks)
    def _(i):
        q = qkv_ref[i, 0, 0]
        scores = dot(keys, q, NT) * scale
        parts = [
            scores[j * rows : (j + 1) * rows] + bias_ref[slot, i, j] for j in range(blocks)
        ]
        top = jnp.max(functools.reduce(jnp.maximum, parts), axis=0, keepdims=True)
        parts = [jnp.exp(part - top) for part in parts]
        total = jnp.sum(functools.reduce(jnp.add, parts), axis=0, keepdims=True)
        inverse = 1.0 / total
        low = jnp.concatenate([(part * inverse).astype(BF16) for part in parts], axis=0)
        out_ref[i, 0] = dot(low, values, TN).astype(BF16)
        lse_ref[0, pl.ds(i, 1), :] = top + jnp.log(total)


def backward_kernel(scale, bias_ref, qkv_ref, out_in_ref, lse_ref, grad_ref, out_ref, dk_ref, dv_ref):
    blocks, rows, dim = qkv_ref.shape[0], qkv_ref.shape[3], qkv_ref.shape[4]
    keys = qkv_ref[:, 0, 1].reshape(blocks * rows, dim)
    values = qkv_ref[:, 0, 2].reshape(blocks * rows, dim)
    slot = pl.program_id(0)
    dk_ref[...] = jnp.zeros_like(dk_ref)
    dv_ref[...] = jnp.zeros_like(dv_ref)

    @pl.loop(0, blocks)
    def _(i):
        q = qkv_ref[i, 0, 0]
        g = grad_ref[0, pl.ds(pl.multiple_of(i * rows, rows), rows), :]
        product = g.astype(F32) * out_in_ref[i, 0].astype(F32)
        delta = jnp.sum(product.T, axis=0, keepdims=True)
        lse = lse_ref[0, pl.ds(i, 1), :]
        scores = dot(keys, q, NT) * scale
        prob_grad = dot(values, g, NT)
        lows, grads = [], []
        for j in range(blocks):
            part = slice(j * rows, (j + 1) * rows)
            prob = jnp.exp(scores[part] + (bias_ref[slot, i, j] - lse))
            lows.append(prob.astype(BF16))
            grads.append((prob * (prob_grad[part] - delta) * scale).astype(BF16))
        low = jnp.concatenate(lows, axis=0)
        score_grad = jnp.concatenate(grads, axis=0)
        dv_ref[...] += dot(low, g, NN)
        dk_ref[...] += dot(score_grad, q, NN)
        out_ref[i, 0, 0] = dot(score_grad, keys, TN).astype(BF16)

    out_ref[:, 0, 1] = dk_ref[...].astype(BF16).reshape(blocks, rows, dim)
    out_ref[:, 0, 2] = dv_ref[...].astype(BF16).reshape(blocks, rows, dim)


def tokens_kernel(heads, slot_ref, *refs):
    count = len(refs) // 2
    dim = refs[0].shape[-1]
    for source, target in zip(refs[:count], refs[count:]):
        for h in range(heads):
            target[0, :, h * dim : (h + 1) * dim] = source[slot_ref[h]]


SMEM = pl.BlockSpec(memory_space=pltpu.SMEM)
VMEM = pl.BlockSpec(memory_space=pltpu.VMEM)
PARAMS = pltpu.CompilerParams(vmem_limit_bytes=48 * 1024 * 1024)


def on_device(query_tok, key_tok, value_tok, grad_out, out_weight, block_mask, head_owner):
    seq = lax.axis_size("seq")
    dps = lax.axis_size("dp")
    most, dim, part_width = out_weight.shape
    rows = query_tok.shape[1]
    heads = block_mask.shape[0]
    tiles = block_mask.shape[1]
    length = seq * rows
    width = grad_out.shape[2]
    scale = dim ** (-0.5)
    grad_scale = (dps * length) ** (-0.5)
    slots = slot_numbers(head_owner, most)
    table = slots[:, None] == jnp.arange(seq * most, dtype=jnp.int32)[None, :]
    select = table.astype(BF16)
    mine = lax.dynamic_slice_in_dim(table, lax.axis_index("seq") * most, most, 1)
    used = jnp.any(mine, axis=0)
    kept = jnp.any(
        jnp.logical_and(mine[:, :, None, None], block_mask[:, None] > 0), axis=0
    ) | jnp.logical_not(used)[:, None, None]
    bias = jnp.where(kept, 0.0, -jnp.inf).astype(F32)

    def to_slots(tensor):
        split = tensor[0].reshape(rows, heads, dim)
        spread = jnp.einsum("thd,hj->jtd", split, select, preferred_element_type=F32)
        return spread.astype(BF16).reshape(seq, most, 1, rows, dim)

    dy = lax.all_gather(grad_out, "seq", axis=1, tiled=True)[0]
    sent = jnp.concatenate([to_slots(t) for t in (query_tok, key_tok, value_tok)], axis=2)
    qkv = lax.all_to_all(sent, "seq", split_axis=0, concat_axis=0, tiled=True)
    weight_full = lax.all_gather(out_weight, "dp", axis=2, tiled=True)

    qkv_spec = pl.BlockSpec((seq, 1, 3, rows, dim), lambda s: (0, s, 0, 0, 0))
    out_spec = pl.BlockSpec((seq, 1, rows, dim), lambda s: (0, s, 0, 0))
    lse_spec = pl.BlockSpec((1, tiles, rows), lambda s: (s, 0, 0))
    slot_out, lse = pl.pallas_call(
        functools.partial(forward_kernel, scale),
        grid=(most,),
        out_shape=(
            jax.ShapeDtypeStruct((seq, most, rows, dim), BF16),
            jax.ShapeDtypeStruct((most, tiles, rows), F32),
        ),
        in_specs=[SMEM, qkv_spec],
        out_specs=(out_spec, lse_spec),
        compiler_params=PARAMS,
        name="attention_forward",
    )(bias, qkv)
    out_back = lax.all_to_all(slot_out, "seq", split_axis=0, concat_axis=0, tiled=True)

    grad_attn = jnp.einsum("td,shd->sth", dy, weight_full, preferred_element_type=F32).astype(BF16)
    grads = pl.pallas_call(
        functools.partial(backward_kernel, scale),
        grid=(most,),
        out_shape=jax.ShapeDtypeStruct((seq, most, 3, rows, dim), BF16),
        in_specs=[
            SMEM,
            qkv_spec,
            out_spec,
            lse_spec,
            pl.BlockSpec((1, length, dim), lambda s: (s, 0, 0)),
        ],
        out_specs=qkv_spec,
        scratch_shapes=[pltpu.VMEM((length, dim), F32), pltpu.VMEM((length, dim), F32)],
        compiler_params=PARAMS,
        name="attention_backward",
    )(bias, qkv, slot_out, lse, grad_attn)
    grads_back = lax.all_to_all(grads, "seq", split_axis=0, concat_axis=0, tiled=True)

    weight_total = jnp.einsum(
        "asth,atd->shd", slot_out.reshape(seq, most, rows, dim), dy.reshape(seq, rows, width),
        preferred_element_type=F32,
    )
    weight_low = (weight_total * grad_scale).astype(BF16).reshape(most, dim, dps, part_width)
    weight_parts = lax.all_to_all(
        weight_low.transpose(2, 0, 1, 3), "dp", split_axis=0, concat_axis=0, tiled=True
    )
    weight_grad = jnp.sum(weight_parts.astype(F32), axis=0)
    weight_grad = jnp.where(used[:, None, None], weight_grad, 0.0)

    token_shape = jax.ShapeDtypeStruct((1, rows, heads * dim), BF16)
    flat = (seq * most, rows, dim)
    attn_out, query_grad, key_grad, value_grad = pl.pallas_call(
        functools.partial(tokens_kernel, heads),
        out_shape=(token_shape,) * 4,
        in_specs=[SMEM] + [VMEM] * 4,
        out_specs=(VMEM,) * 4,
        compiler_params=PARAMS,
        name="heads_to_tokens",
    )(
        slots,
        out_back.reshape(flat),
        grads_back[:, :, 0].reshape(flat),
        grads_back[:, :, 1].reshape(flat),
        grads_back[:, :, 2].reshape(flat),
    )
    return (attn_out, query_grad, key_grad, value_grad, weight_grad)


def solution(mesh):
    placed = (
        P("dp", "seq", None),
        P("dp", "seq", None),
        P("dp", "seq", None),
        P("dp", "seq", None),
        P("seq", None, "dp"),
        P(),
        P(),
    )
    return jax.shard_map(
        on_device,
        mesh=mesh,
        in_specs=placed,
        out_specs=(
            P("dp", "seq", None),
            P("dp", "seq", None),
            P("dp", "seq", None),
            P("dp", "seq", None),
            P("seq", None, "dp"),
        ),
        check_vma=False,
    )
```

profile of v0, /device:TPU:0, one launch (start us, length us, event | category | flops | bytes accessed | tf_op | source)
XLA Modules:
  0.0 363.4 jit_solution(240751034142991817)
XLA Ops:
  7.2 0.0 copy-start.5
  7.2 0.0 all-gather.5.cloned.1.call-start
  7.2 0.7 all-gather.5.cloned.1.call-update
  7.9 1.4 copy.46
  9.3 0.0 copy-start.2
  9.3 0.4 copy.47
  9.8 0.0 copy-done.5
  9.8 0.2 convert_reduce_fusion.1
  10.0 0.4 convolution_convert_fusion.2
  10.3 0.2 copy.48
  10.5 0.0 copy-done.2
  10.5 0.3 copy.49
  10.8 0.0 copy-start.3
  10.9 0.4 copy.50
  11.3 0.4 convolution_convert_fusion.1
  11.7 0.2 copy.51
  11.8 0.1 copy-done.3
  11.9 0.3 copy.52
  12.3 0.4 copy.53
  12.7 0.4 convolution_convert_fusion
  13.1 0.2 copy.54
  13.2 1.6 pad_maximum_fusion
  14.9 0.0 copy-start.4
  14.9 6.5 %all-to-all-start = ((bf16[8,3,3,128,128]{4,3,2,1,0:T(8,128)(2,1)}), bf16[8,3,3,128,128]{4,3,2,1,0:T(8,128)(2,1)S(1)}, u32[]{:S(2)}, u32[]{:S(2)}) async-start(bf16[8,3,3,128,128]{4,3,2,1,0:T(8,128)(2,1)} %pad_maximum_fusion), calls=%async_computation | async-start | bytes 4718592 | tf_op jit(solution)/shard_map/all_to_all | solution.py:125
  21.3 0.0 all-gather.3.cloned.1.call-start
  21.4 0.7 all-gather.3.cloned.1.call-update
  22.1 0.1 fusion.16
  22.2 0.0 copy-done.4
  22.3 0.5 and_reduce_fusion
  22.8 0.1 or_select_fusion.bias_ref
  22.8 117.0 %all-to-all-done.qkv_ref = bf16[8,3,3,128,128]{4,3,2,1,0:T(8,128)(2,1)S(1)} async-done(((bf16[8,3,3,128,128]{4,3,2,1,0:T(8,128)(2,1)}), bf16[8,3,3,128,128]{4,3,2,1,0:T(8,128)(2,1)S(1)}, u32[]{:S(2)}, u32[]{:S(2)}) %all-to-all-start) | async-done | bytes 2359328 | tf_op jit(solution)/shard_map/all_to_all | solution.py:125
  139.8 0.0 copy-start
  139.8 18.6 %attention_forward.1 = (bf16[8,3,128,128]{3,2,1,0:T(8,128)(2,1)}, f32[3,8,128]{2,1,0:T(8,128)S(1)}) custom-call(f32[3,8,8]{2,1,0:T(8,128)S(1)} %or_select_fusion.bias_ref, bf16[8,3,3,128,128]{4,3,2,1,0:T(8,128)(2,1)S(1)} %all-to-all-done.qkv_ref), custom_call_target="tpu_custom_call" | custom-call | tf_op jit(solution)/shard_map/attention_forward/pallas_call | solution.py:131
  158.4 3.4 all-gather.5.cloned.1.call-done
  161.9 8.6 %fusion.2 = bf16[3,128,5120]{2,1,0:T(8,128)(2,1)S(1)} fusion(bf16[8,3,128,128]{3,2,1,0:T(8,128)(2,1)} %get-tuple-element.11.out_in_ref, bf16[8,128,5120,1]{2,1,3,0:T(8,128)(2,1)} %bitcast.55), kind=kOutput, calls=%fused_computation.3 | convolution fusion | flops 4030464000 | bytes 15204352 | tf_op jit(solution)/shard_map/asth,atd->shd/dot_general | solution.py:164
  170.4 0.0 copy-done
  170.5 2.3 copy.63
  172.8 5.0 %all-to-all-start.3 = ((bf16[4,3,128,1280]{3,2,1,0:T(8,128)(2,1)}), bf16[4,3,128,1280]{3,2,1,0:T(8,128)(2,1)}, u32[]{:S(2)}, u32[]{:S(2)}) async-start(bf16[4,3,128,1280]{3,2,1,0:T(8,128)(2,1)} %bitcast.53), calls=%async_computation.3 | async-start | bytes 7864320 | tf_op jit(solution)/shard_map/all_to_all | solution.py:169
  177.8 69.3 %all-gather.3.cloned.1.call-done = bf16[3,128,5120]{2,1,0:T(8,128)(2,1)} async-done(((bf16[3,128,1280]{2,1,0:T(8,128)(2,1)}), bf16[3,128,5120]{2,1,0:T(8,128)(2,1)}) %all-gather.3.cloned.1.call-update) | async-done | bytes 3932176 | tf_op jit(solution)/shard_map/all_gather | solution.py:126
  247.0 9.0 %fusion.6.grad_ref = bf16[3,1024,128]{2,1,0:T(8,128)(2,1)S(1)} fusion(bf16[3,128,5120]{2,1,0:T(8,128)(2,1)} %all-gather.3.cloned.1.call-done, bf16[1,1024,5120]{2,1,0:T(8,128)(2,1)} %all-gather.5.cloned.1.call-done), kind=kOutput, calls=%fused_computation.11 | convolution fusion | flops 4026925056 | bytes 15204352 | tf_op jit(solution)/shard_map/td,shd->sth/dot_general | solution.py:145
  256.0 14.4 %attention_backward.1 = bf16[8,3,3,128,128]{4,3,2,1,0:T(8,128)(2,1)S(1)} custom-call(f32[3,8,8]{2,1,0:T(8,128)S(1)} %or_select_fusion.bias_ref, bf16[8,3,3,128,128]{4,3,2,1,0:T(8,128)(2,1)} %copy-done, bf16[8,3,128,128]{3,2,1,0:T(8,128)(2,1)} %get-tuple-element.11.out_in_ref, f32[3,8,128]{2,1,0:T(8,128)S(1)} %get-tuple-element.12.lse_ref, ...), custom_call_target="tpu_custom_call" | custom-call | tf_op jit(solution)/shard_map/attention_backward/pallas_call | solution.py:146
  270.4 0.0 all-to-all-done.3
  270.4 59.2 %all_to_all.20 = bf16[8,3,3,128,128]{4,3,2,1,0:T(8,128)(2,1)} all-to-all(bf16[8,3,3,128,128]{4,3,2,1,0:T(8,128)(2,1)S(1)} %attention_backward.1), channel_id=1, replica_groups=mesh['dp'=4,'seq'=8] {'seq'}, dimensions={0} | all-to-all | bytes 4718592 | tf_op jit(solution)/shard_map/all_to_all | solution.py:162
  329.6 3.5 all-to-all-start.1
  333.2 2.9 convert_reduce_fusion
  336.1 0.0 copy-start.1
  336.1 1.5 broadcast_select_fusion
  337.6 0.8 copy-done.1
  338.4 0.2 fusion.17
  338.6 15.5 %all-to-all-done.1 = bf16[8,3,128,128]{3,2,1,0:T(8,128)(2,1)S(1)} async-done(((bf16[8,3,128,128]{3,2,1,0:T(8,128)(2,1)}), bf16[8,3,128,128]{3,2,1,0:T(8,128)(2,1)S(1)}, u32[]{:S(2)}, u32[]{:S(2)}) %all-to-all-start.1) | async-done | bytes 786464 | tf_op jit(solution)/shard_map/all_to_all | solution.py:143
  354.1 2.5 heads_to_tokens.1
  (4 shorter events, 0.0 us)
Async XLA Ops:
  7.2 2.6 copy-start.5
  7.2 154.7 %all-gather.5.cloned.1.call-start = ((), (), s32[]{:S(2)}) async-start(), calls=%async_computation.5 | async-start | bytes 11796480 | tf_op jit(solution)/shard_map/all_gather | solution.py:123
  9.3 1.2 copy-start.2
  10.8 1.1 copy-start.3
  14.9 7.4 %copy-start.4 = (s32[20,8,8]{0,2,1:T(8,128)S(1)}, s32[20,8,8]{0,2,1:T(8,128)}, u32[]{:S(2)}) copy-start(s32[20,8,8]{0,2,1:T(8,128)} %param.12) | copy-start | bytes 15364
  14.9 125.0 %all-to-all-start = ((bf16[8,3,3,128,128]{4,3,2,1,0:T(8,128)(2,1)}), bf16[8,3,3,128,128]{4,3,2,1,0:T(8,128)(2,1)S(1)}, u32[]{:S(2)}, u32[]{:S(2)}) async-start(bf16[8,3,3,128,128]{4,3,2,1,0:T(8,128)(2,1)} %pad_maximum_fusion), calls=%async_computation | async-start | bytes 4718592 | tf_op jit(solution)/shard_map/all_to_all | solution.py:125
  21.3 225.7 %all-gather.3.cloned.1.call-start = ((), (), s32[]{:S(2)}) async-start(), calls=%async_computation.4 | async-start | bytes 4915200 | tf_op jit(solution)/shard_map/all_gather | solution.py:126
  139.8 30.6 %copy-start = (bf16[8,3,3,128,128]{4,3,2,1,0:T(8,128)(2,1)}, bf16[8,3,3,128,128]{4,3,2,1,0:T(8,128)(2,1)S(1)}, u32[]{:S(2)}) copy-start(bf16[8,3,3,128,128]{4,3,2,1,0:T(8,128)(2,1)S(1)} %all-to-all-done.qkv_ref) | copy-start | bytes 7077892
  172.8 97.6 %all-to-all-start.3 = ((bf16[4,3,128,1280]{3,2,1,0:T(8,128)(2,1)}), bf16[4,3,128,1280]{3,2,1,0:T(8,128)(2,1)}, u32[]{:S(2)}, u32[]{:S(2)}) async-start(bf16[4,3,128,1280]{3,2,1,0:T(8,128)(2,1)} %bitcast.53), calls=%async_computation.3 | async-start | bytes 7864320 | tf_op jit(solution)/shard_map/all_to_all | solution.py:169
  329.6 24.5 %all-to-all-start.1 = ((bf16[8,3,128,128]{3,2,1,0:T(8,128)(2,1)}), bf16[8,3,128,128]{3,2,1,0:T(8,128)(2,1)S(1)}, u32[]{:S(2)}, u32[]{:S(2)}) async-start(bf16[8,3,128,128]{3,2,1,0:T(8,128)(2,1)} %get-tuple-element.11.out_in_ref), calls=%async_computation.1 | async-start | bytes 1572864 | tf_op jit(solution)/shard_map/all_to_all | solution.py:143
  336.1 2.4 copy-start.1
Sparse Core Ops, SparseCore 0:
  9.7 152.1 all-gather.4
  163.7 83.2 all-gather.2
where the time goes:
time: 364 us; the launch traced here: 363 us
  waiting for transfers between devices  207 us (57%)
  blocking collectives  59.2 us (16%)
  Pallas kernels  35.5 us (10%)
  matrix products  18.6 us (5%)
  starting transfers between devices  15 us (4%)
  between operations  14.3 us (4%)
  local copies, waits for them, and re-layouts  7.3 us (2%)
  other arithmetic  6.96 us (2%)
    all_to_all x1, waiting for transfers between devices, on_device(): qkv = lax.all_to_all(sent, 'seq', split_axis=0, concat_axis=0, tiled=True)  117 us
    all_gather x1, waiting for transfers between devices, on_device(): weight_full = lax.all_gather(out_weight, 'dp', axis=2, tiled=True)  69.3 us
    all_to_all x1, blocking collectives, on_device(): lax.all_to_all(grads, 'seq', split_axis=0, concat_axis=0, tiled=True)  59.2 us
    pallas_call x1, Pallas kernels, on_device(): pl.pallas_call(functools.partial(forward_kernel, scale), grid=(most,), ou...  18.6 us
    all_to_all x1, waiting for transfers between devices, on_device(): lax.all_to_all(slot_out, 'seq', split_axis=0, concat_axis=0, tiled=True)  15.5 us
    pallas_call x1, Pallas kernels, on_device(): pl.pallas_call(functools.partial(backward_kernel, scale), grid=(most,), o...  14.4 us
    dot_general x1, matrix products, on_device(): jnp.einsum('td,shd->sth', dy, weight_full, preferred_element_type=F32)  8.96 us
    dot_general x1, matrix products, on_device(): jnp.einsum('asth,atd->shd', slot_out.reshape(seq, most, rows, dim), dy.re...  8.56 us
  transfers between devices with their start and end apart: 5, of which 4 were waited for; matrix products, arithmetic and copies ran while one was open for 9% of the time, Pallas kernels for 9%

commit v1 on v0

--- a/solution.py
+++ b/solution.py
@@ -26,26 +26,180 @@
     return head_owner * most + rank
 
 
-def forward_kernel(scale, bias_ref, qkv_ref, out_ref, lse_ref):
-    blocks, rows, dim = qkv_ref.shape[0], qkv_ref.shape[3], qkv_ref.shape[4]
-    keys = qkv_ref[:, 0, 1].reshape(blocks * rows, dim)
-    values = qkv_ref[:, 0, 2].reshape(blocks * rows, dim)
-    slot = pl.program_id(0)
-
-    @pl.loop(0, blocks)
-    def _(i):
-        q = qkv_ref[i, 0, 0]
-        scores = dot(keys, q, NT) * scale
-        parts = [
-            scores[j * rows : (j + 1) * rows] + bias_ref[slot, i, j] for j in range(blocks)
-        ]
-        top = jnp.max(functools.reduce(jnp.maximum, parts), axis=0, keepdims=True)
-        parts = [jnp.exp(part - top) for part in parts]
-        total = jnp.sum(functools.reduce(jnp.add, parts), axis=0, keepdims=True)
-        inverse = 1.0 / total
-        low = jnp.concatenate([(part * inverse).astype(BF16) for part in parts], axis=0)
-        out_ref[i, 0] = dot(low, values, TN).astype(BF16)
-        lse_ref[0, pl.ds(i, 1), :] = top + jnp.log(total)
+def gather_kernel(
+    scale, bias_ref, sent_ref, dy_ref, weight_ref, qkv_ref, dy_all, out_ref, lse_ref, grad_ref,
+    weight_all, dy_block, own_sem, qkv_send, qkv_recv, weight_send, weight_recv,
+    right_send, left_send, chain_recv, pair_send, pair_recv, load_sem,
+):
+    seq, most, _, rows, dim = qkv_ref.shape
+    dps = weight_all.shape[0]
+    chips = seq // 2
+    me, dp = lax.axis_index("seq"), lax.axis_index("dp")
+    chip, core = me // 2, lax.rem(me, 2)
+    pair = me + 1 - 2 * core
+
+    def remote(source, target, send_sem, recv_sem, where):
+        return pltpu.make_async_remote_copy(
+            src_ref=source, dst_ref=target, send_sem=send_sem, recv_sem=recv_sem,
+            device_id=where, device_id_type=pl.DeviceIdType.MESH,
+        )
+
+    barrier = pltpu.get_barrier_semaphore()
+    for k in range(1, seq):
+        pl.semaphore_signal(
+            barrier, inc=1, device_id=(dp, lax.rem(me + k, seq)), device_id_type=pl.DeviceIdType.MESH
+        )
+    for k in range(1, dps):
+        pl.semaphore_signal(
+            barrier, inc=1, device_id=(lax.rem(dp + k, dps), me), device_id_type=pl.DeviceIdType.MESH
+        )
+    pl.semaphore_wait(barrier, seq - 1 + dps - 1)
+
+    own = [
+        pltpu.make_async_copy(sent_ref.at[me], qkv_ref.at[me], own_sem.at[0]),
+        pltpu.make_async_copy(dy_ref.at[0], dy_all.at[me], own_sem.at[1]),
+        pltpu.make_async_copy(weight_ref, weight_all.at[dp], own_sem.at[2]),
+    ]
+    qkv_copies = []
+    for k in range(1, seq):
+        to = lax.rem(me + k, seq)
+        qkv_copies.append(
+            remote(sent_ref.at[to], qkv_ref.at[me], qkv_send.at[k], qkv_recv.at[k], (dp, to))
+        )
+    weight_copies = [
+        remote(weight_ref, weight_all.at[dp], weight_send.at[k], weight_recv.at[k],
+               (lax.rem(dp + k, dps), me))
+        for k in range(1, dps)
+    ]
+
+    def right_copy(source, origin):
+        return remote(source, dy_all.at[2 * origin + core], right_send.at[origin],
+                      chain_recv.at[origin], (dp, me + 2))
+
+    def left_copy(source, origin):
+        return remote(source, dy_all.at[2 * origin + core], left_send.at[origin],
+                      chain_recv.at[origin], (dp, me - 2))
+
+    def pair_copy(source, origin):
+        return remote(source, dy_all.at[2 * origin + core], pair_send.at[origin],
+                      pair_recv.at[origin], (dp, pair))
+
+    for copy in qkv_copies + weight_copies + own:
+        copy.start()
+
+    @pl.when(chip + 1 < chips)
+    def _():
+        right_copy(dy_ref.at[0], chip).start()
+
+    @pl.when(chip > 0)
+    def _():
+        left_copy(dy_ref.at[0], chip).start()
+
+    pair_copy(dy_ref.at[0], chip).start()
+
+    def pass_on(step):
+        @pl.when(chip - 1 - step >= 0)
+        def _():
+            origin = chip - 1 - step
+            block = dy_all.at[2 * origin + core]
+            right_copy(block, origin).wait_recv()
+
+            @pl.when(chip + 1 < chips)
+            def _():
+                right_copy(block, origin).start()
+
+            pair_copy(block, origin).start()
+
+        @pl.when(chip + 1 + step < chips)
+        def _():
+            origin = chip + 1 + step
+            block = dy_all.at[2 * origin + core]
+            left_copy(block, origin).wait_recv()
+
+            @pl.when(chip > 0)
+            def _():
+                left_copy(block, origin).start()
+
+            pair_copy(block, origin).start()
+
+    for copy in qkv_copies:
+        copy.wait_recv()
+    own[0].wait()
+
+    def forward(slot):
+        keys = qkv_ref[:, slot, 1].reshape(seq * rows, dim)
+        values = qkv_ref[:, slot, 2].reshape(seq * rows, dim)
+
+        @pl.loop(0, seq)
+        def _(i):
+            q = qkv_ref[i, slot, 0]
+            scores = dot(keys, q, NT) * scale
+            parts = [
+                scores[j * rows : (j + 1) * rows] + bias_ref[slot, i, j] for j in range(seq)
+            ]
+            top = jnp.max(functools.reduce(jnp.maximum, parts), axis=0, keepdims=True)
+            parts = [jnp.exp(part - top) for part in parts]
+            total = jnp.sum(functools.reduce(jnp.add, parts), axis=0, keepdims=True)
+            inverse = 1.0 / total
+            low = jnp.concatenate([(part * inverse).astype(BF16) for part in parts], axis=0)
+            out_ref[i, slot] = dot(low, values, TN).astype(BF16)
+            lse_ref[slot, pl.ds(i, 1), :] = top + jnp.log(total)
+
+    def project(block):
+        load = pltpu.make_async_copy(dy_all.at[block], dy_block, load_sem)
+        load.start()
+        load.wait()
+        part_width = weight_all.shape[3]
+        total = None
+        for d in range(dps):
+            term = dot(
+                dy_block[:, d * part_width : (d + 1) * part_width],
+                weight_all[d].reshape(most * dim, part_width), NT,
+            )
+            total = term if total is None else total + term
+        for s in range(most):
+            grad_ref[s, pl.ds(pl.multiple_of(block * rows, rows), rows), :] = total[
+                :, s * dim : (s + 1) * dim
+            ].astype(BF16)
+
+    def project_ring(k):
+        for origin, wanted in (
+            (chip - k, chip - k >= 0),
+            (chip + k, jnp.logical_and(k > 0, chip + k < chips)),
+        ):
+            @pl.when(wanted)
+            def _(origin=origin):
+                project(2 * origin + core)
+                pair_copy(dy_all.at[2 * origin + core], origin).wait_recv()
+                project(2 * origin + 1 - core)
+
+    for step in range(max(chips - 1, most)):
+        if step < most:
+            forward(step)
+        if step < chips - 1:
+            pass_on(step)
+        if step == 0:
+            own[1].wait()
+            own[2].wait()
+            for copy in weight_copies:
+                copy.wait_recv()
+        if step < chips - 1:
+            project_ring(step)
+    project_ring(chips - 1)
+
+    for copy in qkv_copies + weight_copies:
+        copy.wait_send()
+    for origin in range(chips):
+        block = dy_all.at[2 * origin + core]
+        pair_copy(block, origin).wait_send()
+
+        @pl.when(jnp.logical_and(chip + 1 < chips, origin <= chip))
+        def _():
+            right_copy(block, origin).wait_send()
+
+        @pl.when(jnp.logical_and(chip > 0, origin >= chip))
+        def _():
+            left_copy(block, origin).wait_send()
 
 
 def backward_kernel(scale, bias_ref, qkv_ref, out_in_ref, lse_ref, grad_ref, out_ref, dk_ref, dv_ref):
@@ -91,6 +245,7 @@
 
 SMEM = pl.BlockSpec(memory_space=pltpu.SMEM)
 VMEM = pl.BlockSpec(memory_space=pltpu.VMEM)
+ANY = pl.BlockSpec(memory_space=pl.ANY)
 PARAMS = pltpu.CompilerParams(vmem_limit_bytes=48 * 1024 * 1024)
 
 
@@ -120,29 +275,37 @@
         spread = jnp.einsum("thd,hj->jtd", split, select, preferred_element_type=F32)
         return spread.astype(BF16).reshape(seq, most, 1, rows, dim)
 
-    dy = lax.all_gather(grad_out, "seq", axis=1, tiled=True)[0]
     sent = jnp.concatenate([to_slots(t) for t in (query_tok, key_tok, value_tok)], axis=2)
-    qkv = lax.all_to_all(sent, "seq", split_axis=0, concat_axis=0, tiled=True)
-    weight_full = lax.all_gather(out_weight, "dp", axis=2, tiled=True)
-
     qkv_spec = pl.BlockSpec((seq, 1, 3, rows, dim), lambda s: (0, s, 0, 0, 0))
     out_spec = pl.BlockSpec((seq, 1, rows, dim), lambda s: (0, s, 0, 0))
     lse_spec = pl.BlockSpec((1, tiles, rows), lambda s: (s, 0, 0))
-    slot_out, lse = pl.pallas_call(
-        functools.partial(forward_kernel, scale),
-        grid=(most,),
+    chips = seq // 2
+    dma = pltpu.SemaphoreType.DMA
+    qkv, dy, slot_out, lse, grad_attn = pl.pallas_call(
+        functools.partial(gather_kernel, scale),
         out_shape=(
+            jax.ShapeDtypeStruct((seq, most, 3, rows, dim), BF16),
+            jax.ShapeDtypeStruct((seq, rows, width), BF16),
             jax.ShapeDtypeStruct((seq, most, rows, dim), BF16),
             jax.ShapeDtypeStruct((most, tiles, rows), F32),
+            jax.ShapeDtypeStruct((most, length, dim), BF16),
         ),
-        in_specs=[SMEM, qkv_spec],
-        out_specs=(out_spec, lse_spec),
-        compiler_params=PARAMS,
-        name="attention_forward",
-    )(bias, qkv)
+        in_specs=[SMEM, ANY, ANY, ANY],
+        out_specs=(VMEM, ANY, VMEM, VMEM, VMEM),
+        scratch_shapes=[
+            pltpu.VMEM((dps, most, dim, part_width), BF16),
+            pltpu.VMEM((rows, width), BF16),
+            dma((3,)), dma((seq,)), dma((seq,)), dma((dps,)), dma((dps,)),
+            dma((chips,)), dma((chips,)), dma((chips,)), dma((chips,)), dma((chips,)),
+            dma(()),
+        ],
+        compiler_params=pltpu.CompilerParams(
+            vmem_limit_bytes=48 * 1024 * 1024, collective_id=0, has_side_effects=True
+        ),
+        name="gather_forward",
+    )(bias, sent, grad_out, out_weight)
     out_back = lax.all_to_all(slot_out, "seq", split_axis=0, concat_axis=0, tiled=True)
 
-    grad_attn = jnp.einsum("td,shd->sth", dy, weight_full, preferred_element_type=F32).astype(BF16)
     grads = pl.pallas_call(
         functools.partial(backward_kernel, scale),
         grid=(most,),
@@ -159,10 +322,11 @@
         compiler_params=PARAMS,
         name="attention_backward",
     )(bias, qkv, slot_out, lse, grad_attn)
+
+    dy, grads = lax.optimization_barrier((dy, grads))
     grads_back = lax.all_to_all(grads, "seq", split_axis=0, concat_axis=0, tiled=True)
-
     weight_total = jnp.einsum(
-        "asth,atd->shd", slot_out.reshape(seq, most, rows, dim), dy.reshape(seq, rows, width),
+        "asth,atd->shd", slot_out.reshape(seq, most, rows, dim), dy,
         preferred_element_type=F32,
     )
     weight_low = (weight_total * grad_scale).astype(BF16).reshape(most, dim, dps, part_width)

time: 364 us -> 327 us (0.90)
  waiting for transfers between devices: 207 us -> 15.5 us
  Pallas kernels: 35.5 us -> 176 us
  blocking collectives: 59.2 us -> 105 us
  between operations: 14.3 us -> 0.83 us
  starting transfers between devices: 15 us -> 3.55 us
  matrix products: 18.6 us -> 9.63 us
    pallas_call x1, Pallas kernels: 18.6 us -> 159 us  [on_device(): pl.pallas_call(functools.partial(gather_kernel, scale), out_shape=(jax.Sh...]
    all_to_all x2 -> x0, waiting for transfers between devices: 117 us -> none  [the longest x1 117 us: on_device(): qkv = lax.all_to_all(sent, 'seq', split_axis=0, concat_axis=0, tiled=True)]
    all_gather x2 -> x0, waiting for transfers between devices: 72.7 us -> none  [the longest x1 69.3 us: on_device(): weight_full = lax.all_gather(out_weight, 'dp', axis=2, tiled=True)]
    all_to_all x0 -> x1, blocking collectives: none -> 46.8 us  [on_device(): lax.all_to_all(weight_low.transpose(2, 0, 1, 3), 'dp', split_axis=0, conc...]
    all_to_all x2 -> x0, starting transfers between devices: 11.4 us -> none  [the longest x1 6.45 us: on_device(): qkv = lax.all_to_all(sent, 'seq', split_axis=0, concat_axis=0, tiled=True)]
    dot_general x2 -> x1, matrix products: 17.5 us -> 8.57 us  [on_device(): jnp.einsum('asth,atd->shd', slot_out.reshape(seq, most, rows, dim), dy, p...]
  transfers between devices with their start and end apart: 5 -> 1, of which waited for: 4 -> 1; matrix products, arithmetic and copies ran while one was open for 9% -> 1% of each run, Pallas kernels for 9% -> 0%
where the time goes in v1:
time: 327 us; the launch traced here: 326 us
  Pallas kernels  176 us (54%)
  blocking collectives  105 us (32%)
  waiting for transfers between devices  15.5 us (5%)
  other arithmetic  10.2 us (3%)
  matrix products  9.63 us (3%)
  local copies, waits for them, and re-layouts  6.22 us (2%)
  starting transfers between devices  3.55 us (1%)
    pallas_call x1, Pallas kernels, on_device(): pl.pallas_call(functools.partial(gather_kernel, scale), out_shape=(jax.Sh...  159 us
    all_to_all x1, blocking collectives, on_device(): lax.all_to_all(grads, 'seq', split_axis=0, concat_axis=0, tiled=True)  58.2 us
    all_to_all x1, blocking collectives, on_device(): lax.all_to_all(weight_low.transpose(2, 0, 1, 3), 'dp', split_axis=0, conc...  46.8 us
    all_to_all x1, waiting for transfers between devices, on_device(): lax.all_to_all(slot_out, 'seq', split_axis=0, concat_axis=0, tiled=True)  15.5 us
    pallas_call x1, Pallas kernels, on_device(): pl.pallas_call(functools.partial(backward_kernel, scale), grid=(most,), o...  14.4 us
    dot_general x1, matrix products, on_device(): jnp.einsum('asth,atd->shd', slot_out.reshape(seq, most, rows, dim), dy, p...  8.57 us
  transfers between devices with their start and end apart: 1, of which 1 were waited for; matrix products, arithmetic and copies ran while one was open for 1% of the time, Pallas kernels for 0%

profile of v1, /device:TPU:0, one launch (start us, length us, event | category | flops | bytes accessed | tf_op | source)
XLA Modules:
  0.0 326.5 jit_solution(10214584620918456371)
XLA Ops:
  0.6 0.9 convert_reduce_fusion.1
  1.5 0.7 multiply_add_fusion.slot_ref
  2.2 0.6 fusion.12
  2.9 0.5 not.7
  3.4 0.8 broadcast_compare_fusion
  4.1 1.4 copy.43
  5.6 0.0 copy-start.3
  5.6 0.4 copy.44
  6.0 0.4 convolution_convert_fusion.2
  6.4 0.2 copy.45
  6.5 0.1 copy-done.3
  6.6 0.3 copy.46
  7.0 0.0 copy-start.4
  7.0 0.4 copy.47
  7.4 0.4 convolution_convert_fusion.1
  7.8 0.2 copy.48
  8.0 0.1 copy-done.4
  8.1 0.3 copy.49
  8.4 0.0 copy-start.5
  8.4 0.0 copy-start.6
  8.4 0.4 copy.50
  8.9 0.4 convolution_convert_fusion
  9.2 0.2 copy.51
  9.4 0.0 copy-done.5
  9.4 0.5 and_reduce_fusion
  9.9 0.0 copy-done.6
  9.9 0.1 or_select_fusion.bias_ref
  10.0 0.0 copy-start
  10.0 0.0 copy-start.1
  10.0 1.7 pad_maximum_fusion.sent_ref
  11.7 0.0 copy-done
  11.7 0.8 copy-done.1
  12.4 158.7 %gather_forward.1 = (bf16[8,3,3,128,128]{4,3,2,1,0:T(8,128)(2,1)}, bf16[8,128,5120]{2,1,0:T(8,128)(2,1)}, bf16[8,3,128,128]{3,2,1,0:T(8,128)(2,1)}, f32[3,8,128]{2,1,0:T(8,128)S(1)}, bf16[3,1024,128]{2,1,0:T(8,128)(2,1)S(1)}) custom-call(f32[3,8,8]{2,1,0:T(8,128)S(1)} %or_select_fusion.bias_ref, bf16[8,3,3,128,128]{4,3,2,1,0:T(8,128)(2,1)} %pad_maximum_fusion.sent_ref, ...), custom_call_target="tpu_custom_call" | custom-call | tf_op jit(solution)/shard_map/gather_forward/pallas_call | solution.py:284
  171.2 14.4 %attention_backward.1 = bf16[8,3,3,128,128]{4,3,2,1,0:T(8,128)(2,1)S(1)} custom-call(f32[3,8,8]{2,1,0:T(8,128)S(1)} %or_select_fusion.bias_ref, bf16[8,3,3,128,128]{4,3,2,1,0:T(8,128)(2,1)} %get-tuple-element.18.qkv_ref, bf16[8,3,128,128]{3,2,1,0:T(8,128)(2,1)} %get-tuple-element.16.out_in_ref, f32[3,8,128]{2,1,0:T(8,128)S(1)} %get-tuple-element.19.lse_ref, ...), custom_call_target="tpu_custom_call" | custom-call | tf_op jit(solution)/shard_map/attention_backward/pallas_call | solution.py:309
  185.6 8.6 %fusion.2 = bf16[3,128,5120]{2,1,0:T(8,128)(2,1)S(1)} fusion(bf16[8,3,128,128]{3,2,1,0:T(8,128)(2,1)} %get-tuple-element.16.out_in_ref, bf16[8,128,5120]{2,1,0:T(8,128)(2,1)} %get-tuple-element.26), kind=kOutput, calls=%fused_computation.3 | convolution fusion | flops 4030464000 | bytes 15204352 | tf_op jit(solution)/shard_map/asth,atd->shd/dot_general | solution.py:328
  194.1 0.4 copy.58
  194.5 46.8 %all_to_all.15 = bf16[4,3,128,1280]{3,2,1,0:T(8,128)(2,1)} all-to-all(bf16[4,3,128,1280]{3,2,1,0:T(8,128)(2,1)S(1)} %bitcast.43), channel_id=1, replica_groups=mesh['dp'=4,'seq'=8] {'dp'}, dimensions={0} | all-to-all | bytes 7864320 | tf_op jit(solution)/shard_map/all_to_all | solution.py:333
  241.3 58.2 %all_to_all.16 = bf16[8,3,3,128,128]{4,3,2,1,0:T(8,128)(2,1)} all-to-all(bf16[8,3,3,128,128]{4,3,2,1,0:T(8,128)(2,1)S(1)} %attention_backward.1), channel_id=1, replica_groups=mesh['dp'=4,'seq'=8] {'seq'}, dimensions={0} | all-to-all | bytes 4718592 | tf_op jit(solution)/shard_map/all_to_all | solution.py:327
  299.5 3.5 %all-to-all-start = ((bf16[8,3,128,128]{3,2,1,0:T(8,128)(2,1)}), bf16[8,3,128,128]{3,2,1,0:T(8,128)(2,1)S(1)}, u32[]{:S(2)}, u32[]{:S(2)}) async-start(bf16[8,3,128,128]{3,2,1,0:T(8,128)(2,1)} %get-tuple-element.16.out_in_ref), calls=%async_computation | async-start | bytes 1572864 | tf_op jit(solution)/shard_map/all_to_all | solution.py:307
  303.1 2.9 convert_reduce_fusion
  306.0 0.0 copy-start.2
  306.0 1.5 broadcast_select_fusion
  307.5 0.8 copy-done.2
  308.3 0.2 fusion.13
  308.5 15.5 %all-to-all-done = bf16[8,3,128,128]{3,2,1,0:T(8,128)(2,1)S(1)} async-done(((bf16[8,3,128,128]{3,2,1,0:T(8,128)(2,1)}), bf16[8,3,128,128]{3,2,1,0:T(8,128)(2,1)S(1)}, u32[]{:S(2)}, u32[]{:S(2)}) %all-to-all-start) | async-done | bytes 786464 | tf_op jit(solution)/shard_map/all_to_all | solution.py:307
  323.9 2.5 heads_to_tokens.1
  (1 shorter events, 0.0 us)
Async XLA Ops:
  5.6 1.1 copy-start.3
  7.0 1.1 copy-start.4
  8.4 1.0 copy-start.5
  8.4 1.5 copy-start.6
  10.0 1.7 copy-start
  10.0 2.4 copy-start.1
  299.5 24.5 %all-to-all-start = ((bf16[8,3,128,128]{3,2,1,0:T(8,128)(2,1)}), bf16[8,3,128,128]{3,2,1,0:T(8,128)(2,1)S(1)}, u32[]{:S(2)}, u32[]{:S(2)}) async-start(bf16[8,3,128,128]{3,2,1,0:T(8,128)(2,1)} %get-tuple-element.16.out_in_ref), calls=%async_computation | async-start | bytes 1572864 | tf_op jit(solution)/shard_map/all_to_all | solution.py:307
  306.0 2.4 copy-start.2

commit v2 on v1

--- a/solution.py
+++ b/solution.py
@@ -202,45 +202,133 @@
             left_copy(block, origin).wait_send()
 
 
-def backward_kernel(scale, bias_ref, qkv_ref, out_in_ref, lse_ref, grad_ref, out_ref, dk_ref, dv_ref):
-    blocks, rows, dim = qkv_ref.shape[0], qkv_ref.shape[3], qkv_ref.shape[4]
-    keys = qkv_ref[:, 0, 1].reshape(blocks * rows, dim)
-    values = qkv_ref[:, 0, 2].reshape(blocks * rows, dim)
-    slot = pl.program_id(0)
-    dk_ref[...] = jnp.zeros_like(dk_ref)
-    dv_ref[...] = jnp.zeros_like(dv_ref)
-
-    @pl.loop(0, blocks)
-    def _(i):
-        q = qkv_ref[i, 0, 0]
-        g = grad_ref[0, pl.ds(pl.multiple_of(i * rows, rows), rows), :]
-        product = g.astype(F32) * out_in_ref[i, 0].astype(F32)
-        delta = jnp.sum(product.T, axis=0, keepdims=True)
-        lse = lse_ref[0, pl.ds(i, 1), :]
-        scores = dot(keys, q, NT) * scale
-        prob_grad = dot(values, g, NT)
-        lows, grads = [], []
-        for j in range(blocks):
-            part = slice(j * rows, (j + 1) * rows)
-            prob = jnp.exp(scores[part] + (bias_ref[slot, i, j] - lse))
-            lows.append(prob.astype(BF16))
-            grads.append((prob * (prob_grad[part] - delta) * scale).astype(BF16))
-        low = jnp.concatenate(lows, axis=0)
-        score_grad = jnp.concatenate(grads, axis=0)
-        dv_ref[...] += dot(low, g, NN)
-        dk_ref[...] += dot(score_grad, q, NN)
-        out_ref[i, 0, 0] = dot(score_grad, keys, TN).astype(BF16)
-
-    out_ref[:, 0, 1] = dk_ref[...].astype(BF16).reshape(blocks, rows, dim)
-    out_ref[:, 0, 2] = dv_ref[...].astype(BF16).reshape(blocks, rows, dim)
-
-
-def tokens_kernel(heads, slot_ref, *refs):
-    count = len(refs) // 2
-    dim = refs[0].shape[-1]
-    for source, target in zip(refs[:count], refs[count:]):
-        for h in range(heads):
-            target[0, :, h * dim : (h + 1) * dim] = source[slot_ref[h]]
+def backward_kernel(
+    scale, grad_scale, bias_ref, qkv_ref, out_ref, lse_ref, grad_ref, dy_ref,
+    out_back, grads_back, weight_back,
+    grads_ref, dk_ref, dv_ref, dy_part, weight_part,
+    own_sem, own_grad_sem, out_send, out_recv, grads_send, grads_recv, weight_send, weight_recv, load_sem,
+):
+    seq, most, _, rows, dim = qkv_ref.shape
+    dps, part_width = weight_part.shape[0], weight_part.shape[3]
+    me, dp = lax.axis_index("seq"), lax.axis_index("dp")
+
+    def remote(source, target, send_sem, recv_sem, where):
+        return pltpu.make_async_remote_copy(
+            src_ref=source, dst_ref=target, send_sem=send_sem, recv_sem=recv_sem,
+            device_id=where, device_id_type=pl.DeviceIdType.MESH,
+        )
+
+    def load(k):
+        column = pl.multiple_of(lax.rem(dp + k, dps) * part_width, 128)
+        return pltpu.make_async_copy(
+            dy_ref.at[:, :, pl.ds(column, part_width)], dy_part.at[k % 2], load_sem.at[k % 2]
+        )
+
+    load(1 % dps).start()
+    barrier = pltpu.get_barrier_semaphore()
+    for k in range(1, seq):
+        pl.semaphore_signal(
+            barrier, inc=1, device_id=(dp, lax.rem(me + k, seq)), device_id_type=pl.DeviceIdType.MESH
+        )
+    for k in range(1, dps):
+        pl.semaphore_signal(
+            barrier, inc=1, device_id=(lax.rem(dp + k, dps), me), device_id_type=pl.DeviceIdType.MESH
+        )
+    pl.semaphore_wait(barrier, seq - 1 + dps - 1)
+
+    pending = []
+    own = [pltpu.make_async_copy(out_ref.at[me], out_back.at[me], own_sem.at[0])]
+    own[0].start()
+    for k in range(1, seq):
+        to = lax.rem(me + k, seq)
+        copy = remote(out_ref.at[to], out_back.at[me], out_send.at[k], out_recv.at[k], (dp, to))
+        copy.start()
+        pending.append(copy)
+
+    order = list(range(1, dps)) + [dps]
+    for k in order:
+        part = lax.rem(dp + k, dps)
+        load(k).wait()
+        if k < dps:
+            load(k + 1).start()
+
+        @pl.loop(0, most)
+        def _(slot):
+            rows_out = out_ref[:, slot].reshape(seq * rows, dim)
+            total = dot(rows_out, dy_part[k % 2].reshape(seq * rows, part_width), TN)
+            weight_part[part, slot] = (total * grad_scale).astype(BF16)
+
+        if k < dps:
+            copy = remote(weight_part.at[part], weight_back.at[dp], weight_send.at[k],
+                          weight_recv.at[k], (part, me))
+            pending.append(copy)
+        else:
+            copy = pltpu.make_async_copy(weight_part.at[dp], weight_back.at[dp], own_sem.at[1])
+            own.append(copy)
+        copy.start()
+
+    for slot in range(most):
+        keys = qkv_ref[:, slot, 1].reshape(seq * rows, dim)
+        values = qkv_ref[:, slot, 2].reshape(seq * rows, dim)
+        dk_ref[...] = jnp.zeros_like(dk_ref)
+        dv_ref[...] = jnp.zeros_like(dv_ref)
+
+        @pl.loop(0, seq)
+        def _(i):
+            q = qkv_ref[i, slot, 0]
+            g = grad_ref[slot, pl.ds(pl.multiple_of(i * rows, rows), rows), :]
+            product = g.astype(F32) * out_ref[i, slot].astype(F32)
+            delta = jnp.sum(product.T, axis=0, keepdims=True)
+            lse = lse_ref[slot, pl.ds(i, 1), :]
+            scores = dot(keys, q, NT) * scale
+            prob_grad = dot(values, g, NT)
+            lows, score_grads = [], []
+            for j in range(seq):
+                part = slice(j * rows, (j + 1) * rows)
+                prob = jnp.exp(scores[part] + (bias_ref[slot, i, j] - lse))
+                lows.append(prob.astype(BF16))
+                score_grads.append((prob * (prob_grad[part] - delta) * scale).astype(BF16))
+            low = jnp.concatenate(lows, axis=0)
+            score_grad = jnp.concatenate(score_grads, axis=0)
+            dv_ref[...] += dot(low, g, NN)
+            dk_ref[...] += dot(score_grad, q, NN)
+            grads_ref[i, slot, 0] = dot(score_grad, keys, TN).astype(BF16)
+
+        grads_ref[:, slot, 1] = dk_ref[...].astype(BF16).reshape(seq, rows, dim)
+        grads_ref[:, slot, 2] = dv_ref[...].astype(BF16).reshape(seq, rows, dim)
+        for k in range(1, seq):
+            to = lax.rem(me + k, seq)
+            copy = remote(grads_ref.at[to, slot], grads_back.at[me, slot], grads_send.at[slot, k],
+                          grads_recv.at[slot, k], (dp, to))
+            copy.start()
+            pending.append(copy)
+        copy = pltpu.make_async_copy(
+            grads_ref.at[me, slot], grads_back.at[me, slot], own_grad_sem.at[slot]
+        )
+        copy.start()
+        own.append(copy)
+
+    for copy in own + pending:
+        copy.wait()
+
+
+def tokens_kernel(
+    slot_ref, used_ref, out_ref, grads_ref, weight_ref, attn_out, query_grad, key_grad, value_grad,
+    weight_grad,
+):
+    dim = out_ref.shape[-1]
+    for h in range(slot_ref.shape[0]):
+        columns = slice(h * dim, (h + 1) * dim)
+        slot = slot_ref[h]
+        attn_out[0, :, columns] = out_ref[slot]
+        query_grad[0, :, columns] = grads_ref[slot, 0]
+        key_grad[0, :, columns] = grads_ref[slot, 1]
+        value_grad[0, :, columns] = grads_ref[slot, 2]
+    for s in range(weight_grad.shape[0]):
+        total = functools.reduce(
+            jnp.add, [weight_ref[d, s].astype(F32) for d in range(weight_ref.shape[0])]
+        )
+        weight_grad[s] = jnp.where(used_ref[s] > 0, total, 0.0)
 
 
 SMEM = pl.BlockSpec(memory_space=pltpu.SMEM)
@@ -276,9 +364,6 @@
         return spread.astype(BF16).reshape(seq, most, 1, rows, dim)
 
     sent = jnp.concatenate([to_slots(t) for t in (query_tok, key_tok, value_tok)], axis=2)
-    qkv_spec = pl.BlockSpec((seq, 1, 3, rows, dim), lambda s: (0, s, 0, 0, 0))
-    out_spec = pl.BlockSpec((seq, 1, rows, dim), lambda s: (0, s, 0, 0))
-    lse_spec = pl.BlockSpec((1, tiles, rows), lambda s: (s, 0, 0))
     chips = seq // 2
     dma = pltpu.SemaphoreType.DMA
     qkv, dy, slot_out, lse, grad_attn = pl.pallas_call(
@@ -304,53 +389,44 @@
         ),
         name="gather_forward",
     )(bias, sent, grad_out, out_weight)
-    out_back = lax.all_to_all(slot_out, "seq", split_axis=0, concat_axis=0, tiled=True)
-
-    grads = pl.pallas_call(
-        functools.partial(backward_kernel, scale),
-        grid=(most,),
-        out_shape=jax.ShapeDtypeStruct((seq, most, 3, rows, dim), BF16),
-        in_specs=[
-            SMEM,
-            qkv_spec,
-            out_spec,
-            lse_spec,
-            pl.BlockSpec((1, length, dim), lambda s: (s, 0, 0)),
+    out_back, grads_back, weight_back = pl.pallas_call(
+        functools.partial(backward_kernel, scale, grad_scale),
+        out_shape=(
+            jax.ShapeDtypeStruct((seq, most, rows, dim), BF16),
+            jax.ShapeDtypeStruct((seq, most, 3, rows, dim), BF16),
+            jax.ShapeDtypeStruct((dps, most, dim, part_width), BF16),
+        ),
+        in_specs=[SMEM, VMEM, VMEM, VMEM, VMEM, ANY],
+        out_specs=(ANY,) * 3,
+        scratch_shapes=[
+            pltpu.VMEM((seq, most, 3, rows, dim), BF16),
+            pltpu.VMEM((length, dim), F32),
+            pltpu.VMEM((length, dim), F32),
+            pltpu.VMEM((2, seq, rows, part_width), BF16),
+            pltpu.VMEM((dps, most, dim, part_width), BF16),
+            dma((2,)), dma((most,)), dma((seq,)), dma((seq,)), dma((most, seq)), dma((most, seq)),
+            dma((dps,)), dma((dps,)), dma((2,)),
         ],
-        out_specs=qkv_spec,
-        scratch_shapes=[pltpu.VMEM((length, dim), F32), pltpu.VMEM((length, dim), F32)],
-        compiler_params=PARAMS,
-        name="attention_backward",
-    )(bias, qkv, slot_out, lse, grad_attn)
-
-    dy, grads = lax.optimization_barrier((dy, grads))
-    grads_back = lax.all_to_all(grads, "seq", split_axis=0, concat_axis=0, tiled=True)
-    weight_total = jnp.einsum(
-        "asth,atd->shd", slot_out.reshape(seq, most, rows, dim), dy,
-        preferred_element_type=F32,
-    )
-    weight_low = (weight_total * grad_scale).astype(BF16).reshape(most, dim, dps, part_width)
-    weight_parts = lax.all_to_all(
-        weight_low.transpose(2, 0, 1, 3), "dp", split_axis=0, concat_axis=0, tiled=True
-    )
-    weight_grad = jnp.sum(weight_parts.astype(F32), axis=0)
-    weight_grad = jnp.where(used[:, None, None], weight_grad, 0.0)
+        compiler_params=pltpu.CompilerParams(
+            vmem_limit_bytes=48 * 1024 * 1024, collective_id=1, has_side_effects=True
+        ),
+        name="backward_return",
+    )(bias, qkv, slot_out, lse, grad_attn, dy)
 
     token_shape = jax.ShapeDtypeStruct((1, rows, heads * dim), BF16)
-    flat = (seq * most, rows, dim)
-    attn_out, query_grad, key_grad, value_grad = pl.pallas_call(
-        functools.partial(tokens_kernel, heads),
-        out_shape=(token_shape,) * 4,
-        in_specs=[SMEM] + [VMEM] * 4,
-        out_specs=(VMEM,) * 4,
+    attn_out, query_grad, key_grad, value_grad, weight_grad = pl.pallas_call(
+        tokens_kernel,
+        out_shape=(token_shape,) * 4 + (jax.ShapeDtypeStruct(out_weight.shape, F32),),
+        in_specs=[SMEM, SMEM] + [VMEM] * 3,
+        out_specs=(VMEM,) * 5,
         compiler_params=PARAMS,
         name="heads_to_tokens",
     )(
         slots,
-        out_back.reshape(flat),
-        grads_back[:, :, 0].reshape(flat),
-        grads_back[:, :, 1].reshape(flat),
-        grads_back[:, :, 2].reshape(flat),
+        used.astype(jnp.int32),
+        out_back.reshape(seq * most, rows, dim),
+        grads_back.reshape(seq * most, 3, rows, dim),
+        weight_back,
     )
     return (attn_out, query_grad, key_grad, value_grad, weight_grad)
 

time: 327 us -> 248 us (0.76); the launches traced: 326 us -> 244 us
  blocking collectives: 105 us -> 0 us
  Pallas kernels: 176 us -> 231 us
  waiting for transfers between devices: 15.5 us -> 0 us
  matrix products: 9.63 us -> 1.07 us
  other arithmetic: 10.2 us -> 4.7 us
  starting transfers between devices: 3.55 us -> 0 us
    all_to_all x2 -> x0, blocking collectives: 105 us -> none  [the longest x1 58.2 us: on_device(): lax.all_to_all(grads, 'seq', split_axis=0, concat_axis=0, tiled=True)]
    pallas_call x2, Pallas kernels: 16.9 us -> 72.9 us  [the longest x1 68.2 us: on_device(): pl.pallas_call(functools.partial(backward_kernel, scale, grad_scale), out...]
    all_to_all x1 -> x0, waiting for transfers between devices: 15.5 us -> none  [on_device(): lax.all_to_all(slot_out, 'seq', split_axis=0, concat_axis=0, tiled=True)]
    dot_general x1 -> x0, matrix products: 8.57 us -> none  [on_device(): jnp.einsum('asth,atd->shd', slot_out.reshape(seq, most, rows, dim), dy, p...]
    all_to_all x1 -> x0, starting transfers between devices: 3.55 us -> none  [on_device(): lax.all_to_all(slot_out, 'seq', split_axis=0, concat_axis=0, tiled=True)]
  transfers between devices with their start and end apart: 1 -> 0, of which waited for: 1 -> 0; matrix products, arithmetic and copies ran while one was open for 1% -> 0% of each run, Pallas kernels for 0% -> 0%
where the time goes in v2:
time: 248 us; the launch traced here: 244 us
  Pallas kernels  231 us (93%)
  local copies, waits for them, and re-layouts  6 us (2%)
  other arithmetic  4.7 us (2%)
    pallas_call x1, Pallas kernels, on_device(): pl.pallas_call(functools.partial(gather_kernel, scale), out_shape=(jax.Sh...  159 us
    pallas_call x1, Pallas kernels, on_device(): pl.pallas_call(functools.partial(backward_kernel, scale, grad_scale), out...  68.2 us

profile of v2, /device:TPU:0, one launch (start us, length us, event | category | flops | bytes accessed | tf_op | source)
XLA Modules:
  0.0 244.0 jit_solution(18281326188278090601)
XLA Ops:
  0.6 0.9 convert_reduce_fusion
  1.5 0.7 multiply_add_fusion.slot_ref
  2.2 0.1 fusion.7
  2.4 0.8 broadcast_compare_fusion
  3.1 0.5 and_reduce_fusion
  3.6 0.1 or_select_fusion.bias_ref
  3.7 1.5 copy.28
  5.2 0.0 copy-start.2
  5.2 0.4 copy.29
  5.6 0.4 convolution_convert_fusion.2
  6.0 0.2 copy.30
  6.2 0.1 copy-done.2
  6.3 0.4 copy.31
  6.6 0.4 copy.32
  7.1 0.4 convolution_convert_fusion.1
  7.5 0.2 copy.33
  7.6 1.5 copy.34
  9.1 0.4 copy.35
  9.5 0.4 convolution_convert_fusion
  9.9 0.2 copy.36
  10.1 0.0 copy-start
  10.1 0.0 copy-start.1
  10.1 1.6 pad_maximum_fusion.sent_ref
  11.7 0.0 copy-done
  11.8 0.8 copy-done.1
  12.5 158.5 %gather_forward.1 = (bf16[8,3,3,128,128]{4,3,2,1,0:T(8,128)(2,1)}, bf16[8,128,5120]{2,1,0:T(8,128)(2,1)}, bf16[8,3,128,128]{3,2,1,0:T(8,128)(2,1)S(1)}, f32[3,8,...) custom-call(f32[3,8,8]{2,1,0:T(8,128)S(1)} %or_select_fusion.bias_ref, bf16[8,3,3,128,128]{4,3,2,1,0:T(8,128)(2,1)} %pad_maximum_fusion.sent_ref, ...), custom_call_target="tpu_custom_call" | custom-call | tf_op jit(solution)/shard_map/gather_forward/pallas_call | solution.py:369
  171.0 68.2 %backward_return.1 = (bf16[8,3,128,128]{3,2,1,0:T(8,128)(2,1)S(1)}, bf16[8,3,3,128,128]{4,3,2,1,0:T(8,128)(2,1)S(1)}, bf16[4,3,128,1280]{3,2,1,0:T(8,128)(2,1)}) custom-call(f32[3,8,8]{2,1,0:T(8,128)S(1)} %or_select_fusion.bias_ref, bf16[8,3,3,128,128]{4,3,2,1,0:T(8,128)(2,1)} %get-tuple-element.13.qkv_ref, ...), custom_call_target="tpu_custom_call" | custom-call | tf_op jit(solution)/shard_map/backward_return/pallas_call | solution.py:392
  239.2 4.7 %heads_to_tokens.1 = (bf16[1,128,2560]{2,1,0:T(8,128)(2,1)}, bf16[1,128,2560]{2,1,0:T(8,128)(2,1)}, bf16[1,128,2560]{2,1,0:T(8,128)(2,1)}, bf16[1,128,2560]{2,1,0:T(8,128)(2,1)}, f32[3,128,1280]{2,1,0:T(8,128)}) custom-call(s32[20]{0:T(128)S(1)} %multiply_add_fusion.slot_ref, s32[3]{0:T(128)S(1)} %get-tuple-element.24.used_ref, ...), custom_call_target="tpu_custom_call" | custom-call | tf_op jit(solution)/shard_map/heads_to_tokens/pallas_call | solution.py:417
  (2 shorter events, 0.0 us)
Async XLA Ops:
  5.2 1.1 copy-start.2
  10.1 1.7 copy-start
  10.1 2.4 %copy-start.1 = (bf16[3,128,1280]{2,1,0:T(8,128)(2,1)S(1)}, bf16[3,128,1280]{2,1,0:T(8,128)(2,1)}, u32[]{:S(2)}) copy-start(bf16[3,128,1280]{2,1,0:T(8,128)(2,1)} %weight_ref.1) | copy-start | bytes 2949124
